TPU v7x, 512 devices: a whole 4x8x8 slice. The times are simulated.
512 devices in a mesh: group: 16 (over x_hi, z), member: 32 (over y, x_lo, core).
Axes of the slice: x: 4 (x_hi: 2, x_lo: 2; x = x_hi * 2 + x_lo), y: 8, z: 8, core: 2. Of those that a mesh axis runs over, the one named last changes fastest.
Arguments:
- points: bfloat16 [9, 524288], P(None, ('group', 'member')), may hold values from -4 to 4
- probes: bfloat16 [8, 524288], P(None, ('group', 'member')), may hold values from -40 to 40
- col_blocks: int32 [16, 32, 20], P('group', 'member'), may hold values from 0 to 31, as said below
Outputs:
- product_out: float32 [8, 524288], P(None, ('group', 'member'))
- curvature_out: float32 [8], replicated
Inputs may be any that keep to these rules, and one draw needn't show every extreme that they name: `col_blocks`: the 20 numbers of each row of the last dimension are different.
All inputs are finite; a program needn't handle non-finite values.
Results may differ from a plain program's by a relative error of at most 0.0027.
Values may be sent and summed in bfloat16 or wider, within the bound.
A program may use at most 64 MiB of HBM per device.

v0:
```python
import jax
import jax.numpy as jnp
from jax import lax
from jax.sharding import PartitionSpec as P

noise_level = 3.0
half_inverse = 1.0 / 6.0


def passed_along(block, axis, distance):
    devices = range(lax.axis_size(axis))
    route = [((i - distance) % len(devices), i) for i in devices]
    return lax.ppermute(block, axis, route)


def tile_kernel(row_coords, row_norms, col_coords, col_norms):
    cross_terms = lax.dot_general(
        row_coords, col_coords, (((0,), (0,)), ((), ())), preferred_element_type=jnp.float32
    )
    distance = row_norms[:, None] + col_norms[None, :] - 2.0 * cross_terms
    return jnp.exp(-half_inverse * distance).astype(jnp.bfloat16)


def global_total(local_sums):
    return lax.psum(local_sums, ("group", "member"))


def body(points, probes, col_blocks):
    shard_width = points.shape[1]
    point_dims = points.shape[0]
    member_count = lax.axis_size("member")
    group_count = lax.axis_size("group")
    own_coords = points.astype(jnp.float32)
    own_norms = jnp.sum(own_coords * own_coords, 0)
    stacked = jnp.concatenate((points, probes), 0)
    panel_data = lax.all_gather(stacked, "member", axis=1, tiled=True)
    panel_data = passed_along(panel_data, "group", -1)
    self_tile = tile_kernel(points, own_norms, points, own_norms)
    probe_values = probes.astype(jnp.float32)
    own_terms = noise_level * probe_values + lax.dot_general(
        probes, self_tile, (((1,), (1,)), ((), ())), preferred_element_type=jnp.float32
    )
    listed = col_blocks[0, 0]

    def visit_tile(tile_step, state_pair):
        near_terms, returned = state_pair
        col_start = listed[tile_step] * shard_width
        col_piece = lax.dynamic_slice_in_dim(panel_data, col_start, shard_width, 1)
        far_points = col_piece[:point_dims]
        far_coords = far_points.astype(jnp.float32)
        kernel_block = tile_kernel(
            points, own_norms, far_points, jnp.sum(far_coords * far_coords, 0)
        )
        near_terms = near_terms + lax.dot_general(
            col_piece[point_dims:],
            kernel_block,
            (((1,), (1,)), ((), ())),
            preferred_element_type=jnp.float32,
        )
        back_terms = lax.dot_general(
            probes, kernel_block, (((1,), (0,)), ((), ())), preferred_element_type=jnp.float32
        )
        old_block = lax.dynamic_slice_in_dim(returned, col_start, shard_width, 1)
        returned = lax.dynamic_update_slice_in_dim(returned, old_block + back_terms, col_start, 1)
        return (near_terms, returned)

    start_near = jnp.zeros((probes.shape[0], shard_width), jnp.float32)
    start_back = jnp.zeros((probes.shape[0], shard_width * member_count), jnp.float32)
    near_terms, returned = lax.fori_loop(0, listed.shape[0], visit_tile, (start_near, start_back))
    inverse_count = 1.0 / (shard_width * group_count * member_count)
    moved_back = passed_along(returned, "group", 1)
    share_terms = lax.psum_scatter(moved_back, "member", scatter_dimension=1, tiled=True)
    product_out = own_terms + near_terms + share_terms
    curvature_out = global_total(jnp.sum(probe_values * product_out, 1)) * inverse_count
    return (product_out, curvature_out)


def solution(mesh):
    return jax.shard_map(
        body,
        mesh=mesh,
        in_specs=(
            P(None, ("group", "member")),
            P(None, ("group", "member")),
            P("group", "member", None),
        ),
        out_specs=(P(None, ("group", "member")), P()),
        check_vma=False,
    )
```

profile of v0, /device:TPU:1, one launch (start us, length us, event | category | flops | bytes accessed | tf_op | source)
XLA Modules:
  0.0 504.3 jit_solution(15087547984134171268)
XLA Ops:
  8.7 74.1 %all-gather.2.cloned.1.call-done = bf16[17,32768]{1,0:T(8,128)(2,1)} async-done(((bf16[17,1024]{1,0:T(8,128)(2,1)}), bf16[17,32768]{1,0:T(8,128)(2,1)}) %all-gather.2.cloned.1.call-update) | async-done | bytes 1114128 | tf_op jit(solution)/shard_map/all_gather | solution.py:36
  82.8 7.7 %collective-permute-start = (bf16[17,32768]{1,0:T(8,128)(2,1)}, bf16[17,32768]{1,0:T(8,128)(2,1)}, u32[]{:S(2)}, u32[]{:S(2)}) collective-permute-start(bf16[17,32768]{1,0:T(8,128)(2,1)} %all-gather.2.cloned.1.call-done), channel_id=1, source_target_pairs={{32,0},{64,32},{96,64},{128,96},{160,128},{192,160},{224,192},{256... | collective-permute-start | bytes 3342344 | tf_op jit(solution)/shard_map/ppermute | solution.py:13
  91.3 33.0 %collective-permute-done = bf16[17,32768]{1,0:T(8,128)(2,1)} collective-permute-done((bf16[17,32768]{1,0:T(8,128)(2,1)}, bf16[17,32768]{1,0:T(8,128)(2,1)}, u32[]{:S(2)}, u32[]{:S(2)}) %collective-permute-start) | collective-permute-done | bytes 1114144 | tf_op jit(solution)/shard_map/ppermute | solution.py:13
  124.4 128.6 %while.16 = (s32[]{:T(128)}, f32[8,1024]{1,0:T(8,128)S(1)}, f32[8,32768]{1,0:T(8,128)S(1)}, s32[20]{0:T(128)}, bf16[17,32768]{1,0:T(8,128)(2,1)}, /*index=5*/f32...) while((s32[]{:T(128)}, f32[8,1024]{1,0:T(8,128)S(1)}, ...), condition=%wide.region_3.0_spmd.clone, body=%wide.region_1.0_spmd.clone.sunk | while | flops 57722884 | bytes 6617341 | solution.py:69
  127.1 1.9 fusion.35
  133.5 1.9 fusion.35
  146.4 1.9 fusion.35
  152.8 1.9 fusion.35
  165.7 1.9 fusion.35
  172.1 1.9 fusion.35
  178.5 1.9 fusion.35
  185.0 1.9 fusion.35
  191.4 1.9 fusion.35
  204.2 1.9 fusion.35
  210.7 1.9 fusion.35
  223.5 1.9 fusion.35
  230.0 1.9 fusion.35
  242.8 1.9 fusion.35
  249.2 1.9 fusion.35
  253.0 1.9 collective-permute-start.1
  254.9 28.2 %collective-permute-done.1 = f32[8,32768]{1,0:T(8,128)S(1)} collective-permute-done((f32[8,32768]{1,0:T(8,128)S(1)}, f32[8,32768]{1,0:T(8,128)S(1)}, u32[]{:S(2)}, u32[]{:S(2)}) %collective-permute-start.1) | collective-permute-done | bytes 1048608 | tf_op jit(solution)/shard_map/ppermute | solution.py:13
  284.1 2.3 fusion.10
  286.4 108.8 %reduce-scatter.2.cloned.1.call-done = f32[8,1024]{1,0:T(8,128)} async-done(((f32[8,32768]{1,0:T(8,128)}), f32[8,1024]{1,0:T(8,128)}) %reduce-scatter.2.cloned.1.call-update) | async-done | bytes 32784 | tf_op jit(solution)/shard_map/reduce_scatter | solution.py:72
  396.7 100.2 %psum.7 = f32[8]{0:T(128)S(1)} all-reduce(f32[8]{0:T(128)S(1)} %get-tuple-element.187), channel_id=1, replica_groups=mesh['group'=16,'member'=32] {'group','member'}, use_global_device_ids=true, to_apply=%region_6.0 | all-reduce | flops 8 | bytes 64 | tf_op jit(solution)/shard_map/psum | solution.py:25
  (139 shorter events, 92.1 us)
Async XLA Ops:
  7.2 75.7 %all-gather.2.cloned.1.call-start = ((), (), s32[]{:S(2)}) async-start(), calls=%async_computation.1 | async-start | bytes 1622016 | tf_op jit(solution)/shard_map/all_gather | solution.py:36
  8.6 386.6 %reduce-scatter.2.cloned.1.call-start = ((), (), s32[]{:S(2)}) async-start(), calls=%async_computation.2 | async-start | bytes 1081344 | tf_op jit(solution)/shard_map/reduce_scatter | solution.py:72
  82.8 41.5 %collective-permute-start = (bf16[17,32768]{1,0:T(8,128)(2,1)}, bf16[17,32768]{1,0:T(8,128)(2,1)}, u32[]{:S(2)}, u32[]{:S(2)}) collective-permute-start(bf16[17,32768]{1,0:T(8,128)(2,1)} %all-gather.2.cloned.1.call-done), channel_id=1, source_target_pairs={{32,0},{64,32},{96,64},{128,96},{160,128},{192,160},{224,192},{256... | collective-permute-start | bytes 3342344 | tf_op jit(solution)/shard_map/ppermute | solution.py:13
  127.1 1.9 copy-start.1
  133.5 1.9 copy-start.1
  146.4 1.9 copy-start.1
  152.8 1.9 copy-start.1
  159.2 1.9 copy-start.1
  165.7 1.9 copy-start.1
  172.1 1.9 copy-start.1
  178.5 1.9 copy-start.1
  185.0 1.9 copy-start.1
  191.4 1.9 copy-start.1
  197.8 1.9 copy-start.1
  204.2 1.9 copy-start.1
  210.7 1.9 copy-start.1
  217.1 1.9 copy-start.1
  223.5 1.9 copy-start.1
  230.0 1.9 copy-start.1
  236.4 1.9 copy-start.1
  242.8 1.9 copy-start.1
  249.2 1.9 copy-start.1
  253.0 30.1 %collective-permute-start.1 = (f32[8,32768]{1,0:T(8,128)S(1)}, f32[8,32768]{1,0:T(8,128)S(1)}, u32[]{:S(2)}, u32[]{:S(2)}) collective-permute-start(f32[8,32768]{1,0:T(8,128)S(1)} %get-tuple-element.143), channel_id=1, source_target_pairs={{480,0},{0,32},{32,64},{64,96},{96,128},{128,160},{160,192},{192,2... | collective-permute-start | bytes 3145736 | tf_op jit(solution)/shard_map/ppermute | solution.py:13
  284.1 111.1 %copy-start.2 = (bf16[8,1024]{1,0:T(8,128)(2,1)S(1)}, bf16[8,1024]{1,0:T(8,128)(2,1)}, u32[]{:S(2)}) copy-start(bf16[8,1024]{1,0:T(8,128)(2,1)} %get-tuple-element.283) | copy-start | bytes 49156
  (2 other events, 2.9 us)
Sparse Core Ops, SparseCore 0:
  10.2 72.6 all-gather.1
  284.2 110.9 reduce-scatter.1
where the time goes:
time: 509 us; the launch traced here: 504 us
  waiting for transfers between devices  244 us (48%)
  blocking collectives  100 us (20%)
  matrix products  76.5 us (15%)
  local copies, waits for them, and re-layouts  26.1 us (5%)
  other arithmetic  19.8 us (4%)
  between operations  14.1 us (3%)
  loops' own time  13.7 us (3%)
  starting transfers between devices  9.69 us (2%)
    reduce_scatter x1, waiting for transfers between devices, body(): lax.psum_scatter(moved_back, 'member', scatter_dimension=1, tiled=True)  109 us
    psum x1, blocking collectives, global_total(): return lax.psum(local_sums, ('group', 'member'))  100 us
    all_gather x1, waiting for transfers between devices, body(): panel_data = lax.all_gather(stacked, 'member', axis=1, tiled=True)  74.1 us
    ppermute x2, waiting for transfers between devices, passed_along(): return lax.ppermute(block, axis, route)  61.2 us
    dot_general x20, matrix products, tile_kernel(): lax.dot_general(row_coords, col_coords, (((0,), (0,)), ((), ())), preferr...  37.5 us
    dynamic_slice x20, local copies, waits for them, and re-layouts, visit_tile(): col_start = listed[tile_step] * shard_width  24.9 us
    dot_general x20, matrix products, visit_tile(): lax.dot_general(col_piece[point_dims:], kernel_block, (((1,), (1,)), ((),...  23.9 us
    reduce_sum x20, other arithmetic, visit_tile(): jnp.sum(far_coords * far_coords, 0)  15.6 us
  transfers between devices with their start and end apart: 4, of which 4 were waited for; matrix products, arithmetic and copies ran while one was open for 1% of the time, Pallas kernels for 0%

commit v1 on v0

v1 whole, which is shorter than its diff:
```python
import functools

import jax
import jax.numpy as jnp
from jax import lax
from jax.experimental import pallas as pl
from jax.experimental.pallas import tpu as pltpu
from jax.sharding import PartitionSpec as P

MESH = pl.DeviceIdType.MESH
F32 = jnp.float32
BF16 = jnp.bfloat16

noise_level = 3.0
exponent_scale = 1.4426950408889634 / 3.0

QUAD = 4
OFFSETS = (1, -1, 2, -2, 3, -3, 4)


def split3(value):
    high = value.astype(BF16).astype(F32)
    rest = value - high
    mid = rest.astype(BF16).astype(F32)
    return high, mid, rest - mid


def fill_factor(coords, last, dest):
    pieces = coords.astype(F32)
    squares = pieces[8:16] * pieces[8:16]
    high = squares.astype(BF16).astype(F32)
    dest[0:16, :] = coords
    dest[16:32, :] = jnp.concatenate((high, squares - high), 0).astype(BF16)
    ninth = last.astype(F32)
    ninth_sq = ninth * ninth
    ninth_high = ninth_sq.astype(BF16).astype(F32)
    ninth_low = ninth_sq - ninth_high
    row = lax.broadcasted_iota(jnp.int32, (16, 128), 0)
    base = jnp.where((row >= 3) & (row < 6), 1.0, 0.0)
    for q in range(8):
        part = jnp.where(row == 0, ninth[q : q + 1], base)
        part = jnp.where(row == 1, ninth_high[q : q + 1], part)
        part = jnp.where(row == 2, ninth_low[q : q + 1], part)
        dest[32:48, q * 128 : (q + 1) * 128] = part.astype(BF16)


def kernel(
    dims, group_count, points_ref, probes_ref, listed_ref, product_ref, curvature_ref,
    panel, own, near, total, backs, outbox, inbox, row_factor, factor_a, factor_b, tile_a, tile_b,
    inverse, cur_own, cur_in, cur_group, cur_all,
    shift_sem, gather_send, gather_recv, back_send, back_recv, cur_send, cur_recv, all_send, all_recv,
):
    members, tiles, width = panel.shape[0], backs.shape[0] - 1, points_ref.shape[1]
    rows = members // QUAD
    g = lax.axis_index("group")
    m = lax.axis_index("member")
    y, quad = m // QUAD, lax.rem(m, QUAD)
    nxt = lax.rem(g + 1, group_count)
    prv = lax.rem(g + group_count - 1, group_count)
    across = y * QUAD + lax.rem(quad + 2, QUAD)
    mate = y * QUAD + quad + 1 - 2 * lax.rem(quad, 2)

    def at(row, q):
        return lax.rem(row + rows, rows) * QUAD + q

    barrier = pltpu.get_barrier_semaphore()

    def greet(group, member):
        pl.semaphore_signal(barrier, inc=1, device_id={"group": group, "member": member}, device_id_type=MESH)

    for d in OFFSETS:
        greet(g, at(y + d, quad))
    greet(g, across)
    greet(g, mate)

    def greet_group(i, _):
        greet(lax.rem(g + i, group_count), m)
        return 0

    lax.fori_loop(1, group_count, greet_group, 0)

    probe_values = probes_ref[...].astype(F32)
    coords = points_ref[...].astype(F32)
    own[:, :width] = jnp.concatenate((probe_values, coords[:8]), 0).astype(BF16)
    ninth = coords[8:9]
    folded = jnp.concatenate([ninth[:, q * 128 : (q + 1) * 128] for q in range(8)], 0)
    own[:, width:] = jnp.concatenate((folded, jnp.zeros((8, 128), F32)), 0).astype(BF16)

    pl.semaphore_wait(barrier, len(OFFSETS) + 2 + group_count - 1)

    shift = pltpu.make_async_remote_copy(
        src_ref=own, dst_ref=panel.at[m], send_sem=shift_sem, recv_sem=gather_recv.at[m],
        device_id={"group": prv, "member": m}, device_id_type=MESH,
    )
    shift.start()

    squares = coords[:8] * coords[:8]
    norm = -0.5 * (jnp.sum(squares, 0, keepdims=True) + ninth * ninth)
    norm_parts = split3(norm)
    half = jnp.full((1, width), -0.5, F32)
    side = jnp.concatenate(
        (
            jnp.zeros((8, width), F32), coords[:8], jnp.full((16, width), -0.5, F32),
            ninth, half, half, *norm_parts, jnp.zeros((128 - 38, width), F32),
        ), 0,
    )
    row_factor[...] = jnp.transpose(side)[:, :48].astype(BF16)

    backs[tiles] = jnp.zeros(backs.shape[1:], BF16)

    def find(k, _):
        place = jnp.int32(tiles)
        for t in range(tiles):
            place = jnp.where(listed_ref[0, 0, t] == k, t, place)
        inverse[k] = place
        return 0

    lax.fori_loop(0, members, find, 0)

    def exponent(factor, dest):
        dest[...] = jnp.exp2(
            exponent_scale * jnp.dot(row_factor[...], factor[...], preferred_element_type=F32)
        ).astype(BF16)

    fill_factor(own[:, :width], own[:, width:], factor_a)
    exponent(factor_a, tile_a)

    def towards_near(block, tile):
        return lax.dot_general(block, tile[...], (((1,), (1,)), ((), ())), preferred_element_type=F32)

    total[...] = noise_level * probe_values + towards_near(own[0:8, :width], tile_a)
    near[...] = jnp.zeros_like(near)

    def forward(slot, target, sem):
        copy = pltpu.make_async_remote_copy(
            src_ref=panel.at[slot], dst_ref=panel.at[slot],
            send_sem=gather_send.at[sem], recv_sem=gather_recv.at[slot],
            device_id={"group": g, "member": target}, device_id_type=MESH,
        )
        copy.start()

    def arrived(slot):
        pltpu.make_async_copy(panel.at[slot], panel.at[slot], gather_recv.at[slot]).wait()

    arrived(m)
    for i, d in enumerate(OFFSETS):
        forward(m, at(y + d, quad), i)
    lane = len(OFFSETS)
    forward(m, across, lane)
    forward(m, mate, lane + rows)
    for i, d in enumerate(OFFSETS):
        slot = at(y + d, quad)
        arrived(slot)
        forward(slot, across, lane + 1 + i)
        forward(slot, mate, lane + rows + 1 + i)
    far = lax.rem(quad + 2, QUAD)
    for i, d in enumerate((0,) + OFFSETS):
        slot = at(y + d, far)
        arrived(slot)
        forward(slot, mate, lane + 2 * rows + i)
    sibling = quad + 1 - 2 * lax.rem(quad, 2)
    for q in (sibling, lax.rem(sibling + 2, QUAD)):
        for d in (0,) + OFFSETS:
            arrived(at(y + d, q))

    def prepare(t, factor):
        k = listed_ref[0, 0, t]
        block = panel[k]
        fill_factor(block[:, :width], block[:, width:], factor)

    half_width = width // 2

    def products(t, tile):
        k = listed_ref[0, 0, t]
        near[...] += towards_near(panel[k, 0:8, :width], tile)
        back = jnp.dot(own[0:8, :width], tile[...], preferred_element_type=F32)
        backs[t] = jnp.concatenate((back[:, :half_width], back[:, half_width:]), 0).astype(BF16)

    prepare(0, factor_a)
    exponent(factor_a, tile_a)
    prepare(1, factor_b)

    def pair(u, _):
        products(2 * u, tile_a)
        exponent(factor_b, tile_b)
        prepare(2 * u + 2, factor_a)
        products(2 * u + 1, tile_b)
        exponent(factor_a, tile_a)
        prepare(2 * u + 3, factor_b)
        return 0

    lax.fori_loop(0, tiles // 2 - 1, pair, 0)
    products(tiles - 2, tile_a)
    exponent(factor_b, tile_b)
    products(tiles - 1, tile_b)

    weighted = probe_values * (total[...] + 2.0 * near[...])
    local = weighted[:, :128]
    for q in range(1, width // 128):
        local = local + weighted[:, q * 128 : (q + 1) * 128]
    cur_own[...] = local

    def cur_copy(i):
        peer = lax.rem(m + i, members)
        return pltpu.make_async_remote_copy(
            src_ref=cur_own, dst_ref=cur_in.at[i], send_sem=cur_send.at[i], recv_sem=cur_recv.at[i],
            device_id={"group": g, "member": peer}, device_id_type=MESH,
        )

    def all_copy(i):
        return pltpu.make_async_remote_copy(
            src_ref=cur_group, dst_ref=cur_all.at[i], send_sem=all_send.at[i], recv_sem=all_recv.at[i],
            device_id={"group": lax.rem(g + i, group_count), "member": m}, device_id_type=MESH,
        )

    def back_copy(k):
        return pltpu.make_async_remote_copy(
            src_ref=outbox.at[k], dst_ref=inbox.at[m], send_sem=back_send.at[k], recv_sem=back_recv.at[m],
            device_id={"group": nxt, "member": k}, device_id_type=MESH,
        )

    def each(first, last, step):
        def body(i, _):
            step(i)
            return 0

        lax.fori_loop(first, last, body, 0)

    each(1, members, lambda i: cur_copy(i).start())

    def give_back(i):
        k = lax.rem(m + i, members)
        outbox[k] = backs[inverse[k]]
        back_copy(k).start()

    each(0, members, give_back)

    each(1, members, lambda i: cur_copy(i).wait_recv())
    cur_group[...] = lax.fori_loop(1, members, lambda i, s: s + cur_in[i], cur_own[...])
    each(1, group_count, lambda i: all_copy(i).start())

    def returned(i, state):
        k = lax.rem(m - i + members, members)
        pltpu.make_async_copy(inbox.at[k], inbox.at[k], back_recv.at[k]).wait()
        return state + inbox[k].astype(F32)

    share = lax.fori_loop(0, members, returned, jnp.zeros(inbox.shape[1:], F32))
    product_ref[...] = total[...] + near[...] + jnp.concatenate((share[:8], share[8:]), 1)

    each(1, group_count, lambda i: all_copy(i).wait_recv())
    whole = lax.fori_loop(1, group_count, lambda i, s: s + cur_all[i], cur_group[...])
    curvature_ref[...] = jnp.sum(whole, 1, keepdims=True) * (1.0 / (width * members * group_count))

    shift.wait_send()

    def sent(i):
        pltpu.make_async_copy(panel.at[0], panel.at[0], gather_send.at[i]).wait()

    each(0, len(OFFSETS) + 3 * rows, sent)
    each(0, members, lambda k: back_copy(k).wait_send())
    each(1, members, lambda i: cur_copy(i).wait_send())
    each(1, group_count, lambda i: all_copy(i).wait_send())


def body(points, probes, col_blocks):
    width, dims, rhs = points.shape[1], points.shape[0], probes.shape[0]
    members, groups, tiles = lax.axis_size("member"), lax.axis_size("group"), col_blocks.shape[2]
    rows = members // QUAD
    vmem = pl.BlockSpec(memory_space=pltpu.VMEM)
    dma = pltpu.SemaphoreType.DMA
    product, curvature = pl.pallas_call(
        functools.partial(kernel, dims, groups),
        out_shape=(jax.ShapeDtypeStruct((rhs, width), F32), jax.ShapeDtypeStruct((rhs, 1), F32)),
        in_specs=[vmem, vmem, pl.BlockSpec(memory_space=pltpu.SMEM)],
        out_specs=(vmem, vmem),
        scratch_shapes=[
            pltpu.VMEM((members, 16, width + 128), BF16),
            pltpu.VMEM((16, width + 128), BF16),
            pltpu.VMEM((rhs, width), F32),
            pltpu.VMEM((rhs, width), F32),
            pltpu.VMEM((tiles + 1, 16, width // 2), BF16),
            pltpu.VMEM((members, 16, width // 2), BF16),
            pltpu.VMEM((members, 16, width // 2), BF16),
            pltpu.VMEM((width, 48), BF16),
            pltpu.VMEM((48, width), BF16),
            pltpu.VMEM((48, width), BF16),
            pltpu.VMEM((width, width), BF16),
            pltpu.VMEM((width, width), BF16),
            pltpu.SMEM((members,), jnp.int32),
            pltpu.VMEM((rhs, 128), F32),
            pltpu.VMEM((members, rhs, 128), F32),
            pltpu.VMEM((rhs, 128), F32),
            pltpu.VMEM((groups, rhs, 128), F32),
            dma, dma((len(OFFSETS) + 3 * rows,)), dma((members,)),
            dma((members,)), dma((members,)),
            dma((members,)), dma((members,)),
            dma((groups,)), dma((groups,)),
        ],
        compiler_params=pltpu.CompilerParams(
            collective_id=0, has_side_effects=True, vmem_limit_bytes=40 * 2**20
        ),
    )(points, probes, col_blocks)
    return product, curvature[:, 0]


def solution(mesh):
    return jax.shard_map(
        body,
        mesh=mesh,
        in_specs=(
            P(None, ("group", "member")),
            P(None, ("group", "member")),
            P("group", "member", None),
        ),
        out_specs=(P(None, ("group", "member")), P()),
        check_vma=False,
    )
```

time: 509 us -> 88.2 us (0.17)
  waiting for transfers between devices: 244 us -> 0 us
  blocking collectives: 100 us -> 0 us
  Pallas kernels: 0 us -> 83.9 us
  matrix products: 76.5 us -> 0 us
  local copies, waits for them, and re-layouts: 26.1 us -> 2.74 us
  other arithmetic: 19.8 us -> 0.63 us
  loops' own time: 13.7 us -> 0 us
  between operations: 14.1 us -> 0.65 us
  starting transfers between devices: 9.69 us -> 0 us
    reduce_scatter x1 -> x0, waiting for transfers between devices: 109 us -> none  [body(): lax.psum_scatter(moved_back, 'member', scatter_dimension=1, tiled=True)]
    psum x1 -> x0, blocking collectives: 100 us -> none  [global_total(): return lax.psum(local_sums, ('group', 'member'))]
    pallas_call x0 -> x1, Pallas kernels: none -> 83.9 us  [body(): pl.pallas_call(functools.partial(kernel, dims, groups), out_shape=(jax.Sh...]
    dot_general x61 -> x0, matrix products: 76.5 us -> none  [the longest x20 37.5 us: tile_kernel(): lax.dot_general(row_coords, col_coords, (((0,), (0,)), ((), ())), preferr...]
    all_gather x1 -> x0, waiting for transfers between devices: 74.1 us -> none  [body(): panel_data = lax.all_gather(stacked, 'member', axis=1, tiled=True)]
    ppermute x2 -> x0, waiting for transfers between devices: 61.2 us -> none  [passed_along(): return lax.ppermute(block, axis, route)]
    dynamic_slice x20 -> x0, local copies, waits for them, and re-layouts: 24.9 us -> none  [visit_tile(): col_start = listed[tile_step] * shard_width]
    reduce_sum x22 -> x0, other arithmetic: 17.9 us -> none  [the longest x20 15.6 us: visit_tile(): jnp.sum(far_coords * far_coords, 0)]
  transfers between devices with their start and end apart: 4 -> 0, of which waited for: 4 -> 0; matrix products, arithmetic and copies ran while one was open for 1% -> 0% of each run, Pallas kernels for 0% -> 0%
where the time goes in v1:
time: 88.2 us; the launch traced here: 87.9 us
  Pallas kernels  83.9 us (95%)
  local copies, waits for them, and re-layouts  2.74 us (3%)
    pallas_call x1, Pallas kernels, body(): pl.pallas_call(functools.partial(kernel, dims, groups), out_shape=(jax.Sh...  83.9 us
    unnamed x7, local copies, waits for them, and re-layouts  2.74 us

profile of v1, /device:TPU:1, one launch (start us, length us, event | category | flops | bytes accessed | tf_op | source)
XLA Modules:
  0.0 87.9 jit_solution(10192285095001371243)
XLA Ops:
  0.6 0.0 copy-start
  0.6 0.7 copy-done
  1.4 0.0 copy-start.1
  1.4 0.7 copy-done.1
  2.1 0.0 copy-start.2
  2.1 0.7 copy-done.2
  2.8 83.9 %shard_map.50 = (f32[8,1024]{1,0:T(8,128)S(1)}, f32[8,1]{1,0:T(8,128)S(1)}) custom-call(bf16[9,1024]{1,0:T(8,128)(2,1)S(1)} %copy-done, bf16[8,1024]{1,0:T(8,128)(2,1)S(1)} %copy-done.1, s32[1,1,20]{2,1,0:T(1,128)S(1)} %copy-done.2), custom_call_target="tpu_custom_call" | custom-call | tf_op jit(solution)/shard_map/pallas_call | solution.py:271
  86.7 0.6 reduce
  87.3 0.6 copy.6
Async XLA Ops:
  0.6 0.8 copy-start
  1.4 0.7 copy-start.1
  2.1 0.7 copy-start.2

commit v2 on v1

v2 whole, which is shorter than its diff:
```python
import functools

import jax
import jax.numpy as jnp
from jax import lax
from jax.experimental import pallas as pl
from jax.experimental.pallas import tpu as pltpu
from jax.sharding import PartitionSpec as P

MESH = pl.DeviceIdType.MESH
F32 = jnp.float32
BF16 = jnp.bfloat16

noise_level = 3.0
exponent_scale = 1.4426950408889634 / 3.0

QUAD = 4
ORDER = (0, 1, -1, 3, -3, 2, -2, 4)
NEAR = 5


def split3(value):
    high = value.astype(BF16).astype(F32)
    rest = value - high
    mid = rest.astype(BF16).astype(F32)
    return high, mid, rest - mid


def fill_factor(coords, last, dest):
    pieces = coords.astype(F32)
    squares = pieces[8:16] * pieces[8:16]
    high = squares.astype(BF16).astype(F32)
    dest[0:16, :] = coords
    dest[16:32, :] = jnp.concatenate((high, squares - high), 0).astype(BF16)
    ninth = last.astype(F32)
    ninth_sq = ninth * ninth
    ninth_high = ninth_sq.astype(BF16).astype(F32)
    ninth_low = ninth_sq - ninth_high
    row = lax.broadcasted_iota(jnp.int32, (16, 128), 0)
    base = jnp.where((row >= 3) & (row < 6), 1.0, 0.0)
    for q in range(8):
        part = jnp.where(row == 0, ninth[q : q + 1], base)
        part = jnp.where(row == 1, ninth_high[q : q + 1], part)
        part = jnp.where(row == 2, ninth_low[q : q + 1], part)
        dest[32:48, q * 128 : (q + 1) * 128] = part.astype(BF16)


def kernel(
    dims, group_count, points_ref, probes_ref, listed_ref, product_ref, curvature_ref,
    near_panel, far_panel, own, near, total, backs, outbox, inbox, row_factor, factor_a, factor_b, tile_a, tile_b,
    inverse, sequence, cur_own, cur_in, cur_group, cur_all,
    met, gather_send, gather_recv, back_send, back_recv, cur_send, cur_recv, all_send, all_recv,
):
    members, tiles, width = outbox.shape[0], backs.shape[0] - 1, points_ref.shape[1]
    rows = members // QUAD
    close = NEAR * QUAD
    g = lax.axis_index("group")
    m = lax.axis_index("member")
    y, quad = m // QUAD, lax.rem(m, QUAD)
    nxt = lax.rem(g + 1, group_count)
    prv = lax.rem(g + group_count - 1, group_count)
    across = y * QUAD + lax.rem(quad + 2, QUAD)
    mate = y * QUAD + quad + 1 - 2 * lax.rem(quad, 2)

    def at(row, q):
        return lax.rem(row + rows, rows) * QUAD + q

    barrier = pltpu.get_barrier_semaphore()

    def greet(group, member):
        pl.semaphore_signal(barrier, inc=1, device_id={"group": group, "member": member}, device_id_type=MESH)

    greet(nxt, m)
    for d in ORDER[1:]:
        greet(g, at(y + d, quad))
    greet(g, across)
    greet(g, mate)

    probe_values = probes_ref[...].astype(F32)
    coords = points_ref[...].astype(F32)
    own[:, :width] = jnp.concatenate((probe_values, coords[:8]), 0).astype(BF16)
    ninth = coords[8:9]
    folded = jnp.concatenate([ninth[:, q * 128 : (q + 1) * 128] for q in range(8)], 0)
    own[:, width:] = jnp.concatenate((folded, jnp.zeros((8, 128), F32)), 0).astype(BF16)

    across_quad = lax.rem(quad + 2, QUAD)
    mate_quad = quad + 1 - 2 * lax.rem(quad, 2)

    def spot(place, q):
        if place < NEAR:
            return near_panel.at[place * QUAD + q]
        return far_panel.at[(place - NEAR) * QUAD + q]

    shift = pltpu.make_async_remote_copy(
        src_ref=own, dst_ref=spot(0, quad), send_sem=gather_send.at[0], recv_sem=gather_recv.at[quad],
        device_id={"group": prv, "member": m}, device_id_type=MESH,
    )

    def passing(place, q, to_place, to, sem):
        return pltpu.make_async_remote_copy(
            src_ref=spot(place, q), dst_ref=spot(to_place, q),
            send_sem=gather_send.at[sem], recv_sem=gather_recv.at[to_place * QUAD + q],
            device_id={"group": g, "member": to}, device_id_type=MESH,
        )

    def along(place):
        d = ORDER[place]
        seen = place if d == rows // 2 else ORDER.index(-d)
        return passing(0, quad, seen, at(y + d, quad), place)

    def over(place):
        return passing(place, quad, place, across, rows + place)

    def aside(place):
        return passing(place, quad, place, mate, 2 * rows + place)

    def aside_across(place):
        return passing(place, across_quad, place, mate, 3 * rows + place)

    def arrived(place, q):
        passing(place, q, place, mate, 0).wait_recv()

    pl.semaphore_wait(barrier, rows + 2)
    shift.start()

    squares = coords[:8] * coords[:8]
    norm = -0.5 * (jnp.sum(squares, 0, keepdims=True) + ninth * ninth)
    norm_parts = split3(norm)
    half = jnp.full((1, width), -0.5, F32)
    side = jnp.concatenate(
        (
            jnp.zeros((8, width), F32), coords[:8], jnp.full((16, width), -0.5, F32),
            ninth, half, half, *norm_parts, jnp.zeros((128 - 38, width), F32),
        ), 0,
    )
    row_factor[...] = jnp.transpose(side)[:, :48].astype(BF16)

    backs[tiles] = jnp.zeros(backs.shape[1:], BF16)

    def member_at(position):
        place = position // QUAD
        d = jnp.int32(ORDER[0])
        for i in range(1, rows):
            d = jnp.where(place == i, ORDER[i], d)
        return at(y + d, lax.rem(position, QUAD))

    def find(position, count):
        k = member_at(position)
        hit = jnp.int32(0)
        for t in range(tiles):
            hit = jnp.where(listed_ref[0, 0, t] == k, 1, hit)
        inverse[position] = jnp.where(hit == 1, count, tiles)
        return count + hit

    lax.fori_loop(0, members, find, jnp.int32(0))

    def order(t, _):
        position = jnp.int32(0)
        for p in range(members):
            position = jnp.where(inverse[p] == t, p, position)
        sequence[t] = position
        return 0

    lax.fori_loop(0, tiles, order, 0)

    def exponent(factor, dest):
        dest[...] = jnp.exp2(
            exponent_scale * jnp.dot(row_factor[...], factor[...], preferred_element_type=F32)
        ).astype(BF16)

    fill_factor(own[:, :width], own[:, width:], factor_a)
    exponent(factor_a, tile_a)

    def towards_near(block, tile):
        return lax.dot_general(block, tile[...], (((1,), (1,)), ((), ())), preferred_element_type=F32)

    total[...] = noise_level * probe_values + towards_near(own[0:8, :width], tile_a)
    near[...] = jnp.zeros_like(near)

    def spread(places):
        for place in places:
            along(place).start()

    def relay(places):
        for place in places:
            if place > 0:
                arrived(place, quad)
            over(place).start()
            aside(place).start()

    def relay_across(places):
        for place in places:
            arrived(place, across_quad)
            aside_across(place).start()

    def settle(places):
        for place in places:
            arrived(place, mate_quad)
            arrived(place, lax.rem(mate_quad + 2, QUAD))

    arrived(0, quad)
    spread(range(1, NEAR))
    relay(range(NEAR))
    relay_across(range(NEAR))
    settle(range(NEAR))

    def meet(step):
        for group in (g + (1 << step), g + group_count - (1 << step)):
            pl.semaphore_signal(
                met.at[step], inc=1, device_id={"group": lax.rem(group, group_count), "member": m}, device_id_type=MESH
            )

    meet(0)
    spread(range(NEAR, rows))

    def block_near(t):
        return near_panel[jnp.minimum(sequence[t], close - 1)]

    def block_any(t):
        position = sequence[t]
        a = near_panel[jnp.minimum(position, close - 1)]
        b = far_panel[jnp.maximum(position - close, 0)]
        return jnp.where(position < close, a, b)

    def prepare(block, factor):
        fill_factor(block[:, :width], block[:, width:], factor)

    half_width = width // 2

    def add_near(factor, tile):
        near[...] += towards_near(factor[0:8, :], tile)

    def keep_back(t, tile):
        back = jnp.dot(own[0:8, :width], tile[...], preferred_element_type=F32)
        backs[t] = jnp.concatenate((back[:, :half_width], back[:, half_width:]), 0).astype(BF16)

    def products(t, factor, tile):
        add_near(factor, tile)
        keep_back(t, tile)

    def back_copy(position):
        return pltpu.make_async_remote_copy(
            src_ref=outbox.at[position], dst_ref=inbox.at[m],
            send_sem=back_send.at[position], recv_sem=back_recv.at[m],
            device_id={"group": nxt, "member": member_at(position)}, device_id_type=MESH,
        )

    def give_back(position):
        outbox[position] = backs[inverse[position]]
        back_copy(position).start()

    prepare(block_near(0), factor_a)
    exponent(factor_a, tile_a)
    prepare(block_near(1), factor_b)

    def pair(u, block):
        products(2 * u, factor_a, tile_a)
        exponent(factor_b, tile_b)
        prepare(block(2 * u + 2), factor_a)
        products(2 * u + 1, factor_b, tile_b)
        exponent(factor_a, tile_a)
        prepare(block(2 * u + 3), factor_b)
        give_back(2 * u)
        give_back(2 * u + 1)

    early = 3

    def early_pair(u, _):
        pair(u, block_near)
        for step, acts in enumerate(((), (relay,), (relay_across, settle))):

            @pl.when(u == step)
            def _(step=step, acts=acts):
                for act in acts:
                    act(range(NEAR, rows))
                pl.semaphore_wait(met.at[step], 2)
                if step < 2:
                    meet(step + 1)

        return 0

    def late_pair(u, _):
        pair(u, block_any)
        return 0

    lax.fori_loop(0, early, early_pair, 0)
    lax.fori_loop(early, tiles // 2 - 1, late_pair, 0)
    add_near(factor_a, tile_a)
    exponent(factor_b, tile_b)
    add_near(factor_b, tile_b)

    weighted = probe_values * (total[...] + 2.0 * near[...])
    local = weighted[:, :128]
    for q in range(1, width // 128):
        local = local + weighted[:, q * 128 : (q + 1) * 128]
    line = lax.broadcasted_iota(jnp.int32, local.shape, 0)
    lane = lax.broadcasted_iota(jnp.int32, local.shape, 1)
    sums = jnp.where(line == lane, jnp.sum(local, 1, keepdims=True), 0.0)
    cur_own[...] = jnp.sum(sums, 0, keepdims=True)
    cur_in[0] = cur_own[...]

    def cur_copy(i):
        peer = lax.rem(m + i, members)
        return pltpu.make_async_remote_copy(
            src_ref=cur_own, dst_ref=cur_in.at[i], send_sem=cur_send.at[i], recv_sem=cur_recv.at[i],
            device_id={"group": g, "member": peer}, device_id_type=MESH,
        )

    def all_copy(i):
        return pltpu.make_async_remote_copy(
            src_ref=cur_group, dst_ref=cur_all.at[i], send_sem=all_send.at[i], recv_sem=all_recv.at[i],
            device_id={"group": lax.rem(g + i, group_count), "member": m}, device_id_type=MESH,
        )

    def each(first, last, step):
        def body(i, _):
            step(i)
            return 0

        lax.fori_loop(first, last, body, 0)

    each(1, members, lambda i: cur_copy(i).start())

    keep_back(tiles - 2, tile_a)
    keep_back(tiles - 1, tile_b)
    each(tiles - 2, members, give_back)

    each(1, members, lambda i: cur_copy(i).wait_recv())
    cur_group[...] = jnp.sum(cur_in[...], 0)
    cur_all[0] = cur_group[...]
    each(1, group_count, lambda i: all_copy(i).start())

    def returned(i, state):
        k = lax.rem(m - i + members, members)
        pltpu.make_async_copy(inbox.at[k], inbox.at[k], back_recv.at[k]).wait()
        return state + inbox[k].astype(F32)

    share = lax.fori_loop(0, members, returned, jnp.zeros(inbox.shape[1:], F32))
    product_ref[...] = total[...] + near[...] + jnp.concatenate((share[:8], share[8:]), 1)

    each(1, group_count, lambda i: all_copy(i).wait_recv())
    curvature_ref[...] = jnp.sum(cur_all[...], 0) * (1.0 / (width * members * group_count))

    for place in range(rows):
        (along(place) if place else shift).wait_send()
        over(place).wait_send()
        aside(place).wait_send()
        aside_across(place).wait_send()
    each(0, members, lambda p: back_copy(p).wait_send())
    each(1, members, lambda i: cur_copy(i).wait_send())
    each(1, group_count, lambda i: all_copy(i).wait_send())


def body(points, probes, col_blocks):
    width, dims, rhs = points.shape[1], points.shape[0], probes.shape[0]
    members, groups, tiles = lax.axis_size("member"), lax.axis_size("group"), col_blocks.shape[2]
    rows = members // QUAD
    vmem = pl.BlockSpec(memory_space=pltpu.VMEM)
    dma = pltpu.SemaphoreType.DMA
    product, curvature = pl.pallas_call(
        functools.partial(kernel, dims, groups),
        out_shape=(jax.ShapeDtypeStruct((rhs, width), F32), jax.ShapeDtypeStruct((1, 128), F32)),
        in_specs=[vmem, vmem, pl.BlockSpec(memory_space=pltpu.SMEM)],
        out_specs=(vmem, vmem),
        scratch_shapes=[
            pltpu.VMEM((NEAR * QUAD, 16, width + 128), BF16),
            pltpu.VMEM((members - NEAR * QUAD, 16, width + 128), BF16),
            pltpu.VMEM((16, width + 128), BF16),
            pltpu.VMEM((rhs, width), F32),
            pltpu.VMEM((rhs, width), F32),
            pltpu.VMEM((tiles + 1, 16, width // 2), BF16),
            pltpu.VMEM((members, 16, width // 2), BF16),
            pltpu.VMEM((members, 16, width // 2), BF16),
            pltpu.VMEM((width, 48), BF16),
            pltpu.VMEM((48, width), BF16),
            pltpu.VMEM((48, width), BF16),
            pltpu.VMEM((width, width), BF16),
            pltpu.VMEM((width, width), BF16),
            pltpu.SMEM((members,), jnp.int32),
            pltpu.SMEM((tiles,), jnp.int32),
            pltpu.VMEM((1, 128), F32),
            pltpu.VMEM((members, 1, 128), F32),
            pltpu.VMEM((1, 128), F32),
            pltpu.VMEM((groups, 1, 128), F32),
            pltpu.SemaphoreType.REGULAR((3,)), dma((4 * rows,)), dma((members,)),
            dma((members,)), dma((members,)),
            dma((members,)), dma((members,)),
            dma((groups,)), dma((groups,)),
        ],
        compiler_params=pltpu.CompilerParams(
            collective_id=0, has_side_effects=True, vmem_limit_bytes=40 * 2**20
        ),
    )(points, probes, col_blocks)
    return product, curvature[0, :rhs]


def solution(mesh):
    return jax.shard_map(
        body,
        mesh=mesh,
        in_specs=(
            P(None, ("group", "member")),
            P(None, ("group", "member")),
            P("group", "member", None),
        ),
        out_specs=(P(None, ("group", "member")), P()),
        check_vma=False,
    )
```

time: 88.2 us -> 79.4 us (0.900); the launches traced: 87.9 us -> 77.8 us
  Pallas kernels: 83.9 us -> 73.9 us
    pallas_call x1, Pallas kernels: 83.9 us -> 73.9 us  [body(): pl.pallas_call(functools.partial(kernel, dims, groups), out_shape=(jax.Sh...]
where the time goes in v2:
time: 79.4 us; the launch traced here: 77.8 us
  Pallas kernels  73.9 us (93%)
  local copies, waits for them, and re-layouts  3.25 us (4%)
    pallas_call x1, Pallas kernels, body(): pl.pallas_call(functools.partial(kernel, dims, groups), out_shape=(jax.Sh...  73.9 us
    unnamed x7, local copies, waits for them, and re-layouts  2.74 us

profile of v2, /device:TPU:1, one launch (start us, length us, event | category | flops | bytes accessed | tf_op | source)
XLA Modules:
  0.0 77.8 jit_solution(10012036803149396548)
XLA Ops:
  0.6 0.0 copy-start
  0.6 0.7 copy-done
  1.4 0.0 copy-start.1
  1.4 0.7 copy-done.1
  2.1 0.0 copy-start.2
  2.1 0.7 copy-done.2
  2.8 73.9 %shard_map.50 = (f32[8,1024]{1,0:T(8,128)S(1)}, f32[1,128]{1,0:T(1,128)S(1)}) custom-call(bf16[9,1024]{1,0:T(8,128)(2,1)S(1)} %copy-done, bf16[8,1024]{1,0:T(8,128)(2,1)S(1)} %copy-done.1, s32[1,1,20]{2,1,0:T(1,128)S(1)} %copy-done.2), custom_call_target="tpu_custom_call" | custom-call | tf_op jit(solution)/shard_map/pallas_call | solution.py:360
  76.7 0.5 slice_bitcast_fusion
  77.2 0.6 copy.6
Async XLA Ops:
  0.6 0.8 copy-start
  1.4 0.7 copy-start.1
  2.1 0.7 copy-start.2

commit v3 on v2

--- a/solution.py
+++ b/solution.py
@@ -15,7 +15,8 @@
 exponent_scale = 1.4426950408889634 / 3.0
 
 QUAD = 4
-ORDER = (0, 1, -1, 3, -3, 2, -2, 4)
+ORDER = (0, 2, -2, 3, -3, 1, -1, 4)
+HOME = ORDER.index(0)
 NEAR = 5
 
 
@@ -71,8 +72,9 @@
         pl.semaphore_signal(barrier, inc=1, device_id={"group": group, "member": member}, device_id_type=MESH)
 
     greet(nxt, m)
-    for d in ORDER[1:]:
-        greet(g, at(y + d, quad))
+    for d in ORDER:
+        if d != 0:
+            greet(g, at(y + d, quad))
     greet(g, across)
     greet(g, mate)
 
@@ -92,30 +94,30 @@
         return far_panel.at[(place - NEAR) * QUAD + q]
 
     shift = pltpu.make_async_remote_copy(
-        src_ref=own, dst_ref=spot(0, quad), send_sem=gather_send.at[0], recv_sem=gather_recv.at[quad],
+        src_ref=own, dst_ref=spot(HOME, quad), send_sem=gather_send.at[0], recv_sem=gather_recv.at[HOME * QUAD + quad],
         device_id={"group": prv, "member": m}, device_id_type=MESH,
     )
 
-    def passing(place, q, to_place, to, sem):
+    def passing(place, q, to_place, to, sent_with):
         return pltpu.make_async_remote_copy(
             src_ref=spot(place, q), dst_ref=spot(to_place, q),
-            send_sem=gather_send.at[sem], recv_sem=gather_recv.at[to_place * QUAD + q],
+            send_sem=gather_send.at[0 if sent_with < NEAR else 1], recv_sem=gather_recv.at[to_place * QUAD + q],
             device_id={"group": g, "member": to}, device_id_type=MESH,
         )
 
     def along(place):
         d = ORDER[place]
         seen = place if d == rows // 2 else ORDER.index(-d)
-        return passing(0, quad, seen, at(y + d, quad), place)
+        return passing(HOME, quad, seen, at(y + d, quad), place)
 
     def over(place):
-        return passing(place, quad, place, across, rows + place)
+        return passing(place, quad, place, across, place)
 
     def aside(place):
-        return passing(place, quad, place, mate, 2 * rows + place)
+        return passing(place, quad, place, mate, place)
 
     def aside_across(place):
-        return passing(place, across_quad, place, mate, 3 * rows + place)
+        return passing(place, across_quad, place, mate, place)
 
     def arrived(place, q):
         passing(place, q, place, mate, 0).wait_recv()
@@ -135,6 +137,37 @@
     )
     row_factor[...] = jnp.transpose(side)[:, :48].astype(BF16)
 
+    def exponent(factor, dest):
+        dest[...] = jnp.exp2(
+            exponent_scale * jnp.dot(row_factor[...], factor[...], preferred_element_type=F32)
+        ).astype(BF16)
+
+    def spread(places):
+        for place in places:
+            if place != HOME:
+                along(place).start()
+
+    def relay(places):
+        for place in places:
+            if place != HOME:
+                arrived(place, quad)
+            over(place).start()
+            aside(place).start()
+
+    def relay_across(places):
+        for place in places:
+            arrived(place, across_quad)
+            aside_across(place).start()
+
+    def settle(places):
+        for place in places:
+            arrived(place, mate_quad)
+            arrived(place, lax.rem(mate_quad + 2, QUAD))
+
+    arrived(HOME, quad)
+    spread(range(NEAR))
+    relay((HOME,))
+
     backs[tiles] = jnp.zeros(backs.shape[1:], BF16)
 
     def member_at(position):
@@ -163,10 +196,7 @@
 
     lax.fori_loop(0, tiles, order, 0)
 
-    def exponent(factor, dest):
-        dest[...] = jnp.exp2(
-            exponent_scale * jnp.dot(row_factor[...], factor[...], preferred_element_type=F32)
-        ).astype(BF16)
+    relay([place for place in range(NEAR) if place != HOME])
 
     fill_factor(own[:, :width], own[:, width:], factor_a)
     exponent(factor_a, tile_a)
@@ -177,30 +207,6 @@
     total[...] = noise_level * probe_values + towards_near(own[0:8, :width], tile_a)
     near[...] = jnp.zeros_like(near)
 
-    def spread(places):
-        for place in places:
-            along(place).start()
-
-    def relay(places):
-        for place in places:
-            if place > 0:
-                arrived(place, quad)
-            over(place).start()
-            aside(place).start()
-
-    def relay_across(places):
-        for place in places:
-            arrived(place, across_quad)
-            aside_across(place).start()
-
-    def settle(places):
-        for place in places:
-            arrived(place, mate_quad)
-            arrived(place, lax.rem(mate_quad + 2, QUAD))
-
-    arrived(0, quad)
-    spread(range(1, NEAR))
-    relay(range(NEAR))
     relay_across(range(NEAR))
     settle(range(NEAR))
 
@@ -227,21 +233,21 @@
 
     half_width = width // 2
 
-    def add_near(factor, tile):
-        near[...] += towards_near(factor[0:8, :], tile)
+    def add_near(block, tile):
+        near[...] += towards_near(block, tile)
 
     def keep_back(t, tile):
         back = jnp.dot(own[0:8, :width], tile[...], preferred_element_type=F32)
         backs[t] = jnp.concatenate((back[:, :half_width], back[:, half_width:]), 0).astype(BF16)
 
     def products(t, factor, tile):
-        add_near(factor, tile)
+        add_near(factor[0:8, :], tile)
         keep_back(t, tile)
 
     def back_copy(position):
         return pltpu.make_async_remote_copy(
             src_ref=outbox.at[position], dst_ref=inbox.at[m],
-            send_sem=back_send.at[position], recv_sem=back_recv.at[m],
+            send_sem=back_send, recv_sem=back_recv,
             device_id={"group": nxt, "member": member_at(position)}, device_id_type=MESH,
         )
 
@@ -272,7 +278,7 @@
             @pl.when(u == step)
             def _(step=step, acts=acts):
                 for act in acts:
-                    act(range(NEAR, rows))
+                    act([place for place in range(NEAR, rows) if act != relay or place != HOME])
                 pl.semaphore_wait(met.at[step], 2)
                 if step < 2:
                     meet(step + 1)
@@ -285,9 +291,9 @@
 
     lax.fori_loop(0, early, early_pair, 0)
     lax.fori_loop(early, tiles // 2 - 1, late_pair, 0)
-    add_near(factor_a, tile_a)
+    add_near(factor_a[0:8, :], tile_a)
     exponent(factor_b, tile_b)
-    add_near(factor_b, tile_b)
+    add_near(factor_b[0:8, :], tile_b)
 
     weighted = probe_values * (total[...] + 2.0 * near[...])
     local = weighted[:, :128]
@@ -302,13 +308,13 @@
     def cur_copy(i):
         peer = lax.rem(m + i, members)
         return pltpu.make_async_remote_copy(
-            src_ref=cur_own, dst_ref=cur_in.at[i], send_sem=cur_send.at[i], recv_sem=cur_recv.at[i],
+            src_ref=cur_own, dst_ref=cur_in.at[i], send_sem=cur_send, recv_sem=cur_recv,
             device_id={"group": g, "member": peer}, device_id_type=MESH,
         )
 
     def all_copy(i):
         return pltpu.make_async_remote_copy(
-            src_ref=cur_group, dst_ref=cur_all.at[i], send_sem=all_send.at[i], recv_sem=all_recv.at[i],
+            src_ref=cur_group, dst_ref=cur_all.at[i], send_sem=all_send, recv_sem=all_recv,
             device_id={"group": lax.rem(g + i, group_count), "member": m}, device_id_type=MESH,
         )
 
@@ -323,32 +329,36 @@
 
     keep_back(tiles - 2, tile_a)
     keep_back(tiles - 1, tile_b)
-    each(tiles - 2, members, give_back)
-
-    each(1, members, lambda i: cur_copy(i).wait_recv())
+    each(tiles - 2, members, lambda i: give_back(members - 1 + tiles - 2 - i))
+
+
+    def whole(ref, send_sem, recv_sem):
+        return pltpu.make_async_remote_copy(
+            src_ref=ref, dst_ref=ref, send_sem=send_sem, recv_sem=recv_sem,
+            device_id={"group": g, "member": mate}, device_id_type=MESH,
+        )
+
+    rest = pl.ds(1, members - 1)
+    whole(cur_in.at[rest], cur_send, cur_recv).wait_recv()
     cur_group[...] = jnp.sum(cur_in[...], 0)
     cur_all[0] = cur_group[...]
     each(1, group_count, lambda i: all_copy(i).start())
 
-    def returned(i, state):
-        k = lax.rem(m - i + members, members)
-        pltpu.make_async_copy(inbox.at[k], inbox.at[k], back_recv.at[k]).wait()
-        return state + inbox[k].astype(F32)
-
-    share = lax.fori_loop(0, members, returned, jnp.zeros(inbox.shape[1:], F32))
+    whole(near_panel, gather_send.at[0], gather_recv.at[0]).wait_send()
+    whole(far_panel, gather_send.at[1], gather_recv.at[0]).wait_send()
+    whole(cur_in.at[rest], cur_send, cur_recv).wait_send()
+    whole(outbox, back_send, back_recv).wait_send()
+    others = cur_all.at[pl.ds(1, group_count - 1)]
+    whole(others, all_send, all_recv).wait_send()
+
+    whole(inbox, back_send, back_recv).wait_recv()
+    share = inbox[0].astype(F32)
+    for k in range(1, members):
+        share = share + inbox[k].astype(F32)
     product_ref[...] = total[...] + near[...] + jnp.concatenate((share[:8], share[8:]), 1)
 
-    each(1, group_count, lambda i: all_copy(i).wait_recv())
+    whole(others, all_send, all_recv).wait_recv()
     curvature_ref[...] = jnp.sum(cur_all[...], 0) * (1.0 / (width * members * group_count))
-
-    for place in range(rows):
-        (along(place) if place else shift).wait_send()
-        over(place).wait_send()
-        aside(place).wait_send()
-        aside_across(place).wait_send()
-    each(0, members, lambda p: back_copy(p).wait_send())
-    each(1, members, lambda i: cur_copy(i).wait_send())
-    each(1, group_count, lambda i: all_copy(i).wait_send())
 
 
 def body(points, probes, col_blocks):
@@ -374,21 +384,18 @@
             pltpu.VMEM((width, 48), BF16),
             pltpu.VMEM((48, width), BF16),
             pltpu.VMEM((48, width), BF16),
-            pltpu.VMEM((width, width), BF16),
-            pltpu.VMEM((width, width), BF16),
+            *[pltpu.VMEM((width, width), BF16)] * 2,
             pltpu.SMEM((members,), jnp.int32),
             pltpu.SMEM((tiles,), jnp.int32),
             pltpu.VMEM((1, 128), F32),
             pltpu.VMEM((members, 1, 128), F32),
             pltpu.VMEM((1, 128), F32),
             pltpu.VMEM((groups, 1, 128), F32),
-            pltpu.SemaphoreType.REGULAR((3,)), dma((4 * rows,)), dma((members,)),
-            dma((members,)), dma((members,)),
-            dma((members,)), dma((members,)),
-            dma((groups,)), dma((groups,)),
+            pltpu.SemaphoreType.REGULAR((3,)), dma((2,)), dma((members,)),
+            dma, dma, dma, dma, dma, dma,
         ],
         compiler_params=pltpu.CompilerParams(
-            collective_id=0, has_side_effects=True, vmem_limit_bytes=40 * 2**20
+            collective_id=0, has_side_effects=True, vmem_limit_bytes=48 * 2**20
         ),
     )(points, probes, col_blocks)
     return product, curvature[0, :rhs]

time: 79.4 us -> 76.6 us (0.965); the launches traced: 77.8 us -> 76.3 us
  Pallas kernels: 73.9 us -> 72.4 us
    pallas_call x1, Pallas kernels: 73.9 us -> 72.4 us  [body(): pl.pallas_call(functools.partial(kernel, dims, groups), out_shape=(jax.Sh...]
where the time goes in v3:
time: 76.6 us; the launch traced here: 76.3 us
  Pallas kernels  72.4 us (95%)
  local copies, waits for them, and re-layouts  3.25 us (4%)
    pallas_call x1, Pallas kernels, body(): pl.pallas_call(functools.partial(kernel, dims, groups), out_shape=(jax.Sh...  72.4 us
    unnamed x7, local copies, waits for them, and re-layouts  2.74 us

profile of v3, /device:TPU:1, one launch (start us, length us, event | category | flops | bytes accessed | tf_op | source)
XLA Modules:
  0.0 76.3 jit_solution(5414110702045714958)
XLA Ops:
  0.6 0.0 copy-start
  0.6 0.7 copy-done
  1.4 0.0 copy-start.1
  1.4 0.7 copy-done.1
  2.1 0.0 copy-start.2
  2.1 0.7 copy-done.2
  2.8 72.4 %shard_map.50 = (f32[8,1024]{1,0:T(8,128)S(1)}, f32[1,128]{1,0:T(1,128)S(1)}) custom-call(bf16[9,1024]{1,0:T(8,128)(2,1)S(1)} %copy-done, bf16[8,1024]{1,0:T(8,128)(2,1)S(1)} %copy-done.1, s32[1,1,20]{2,1,0:T(1,128)S(1)} %copy-done.2), custom_call_target="tpu_custom_call" | custom-call | tf_op jit(solution)/shard_map/pallas_call | solution.py:370
  75.2 0.5 slice_bitcast_fusion
  75.7 0.6 copy.6
Async XLA Ops:
  0.6 0.8 copy-start
  1.4 0.7 copy-start.1
  2.1 0.7 copy-start.2

commit v4 on v3

--- a/solution.py
+++ b/solution.py
@@ -15,8 +15,9 @@
 exponent_scale = 1.4426950408889634 / 3.0
 
 QUAD = 4
-ORDER = (0, 2, -2, 3, -3, 1, -1, 4)
+ORDER = (2, -2, 3, -3, 0, 1, -1, 4)
 HOME = ORDER.index(0)
+SINGLE = 4
 NEAR = 5
 
 
@@ -48,13 +49,15 @@
 
 def kernel(
     dims, group_count, points_ref, probes_ref, listed_ref, product_ref, curvature_ref,
-    near_panel, far_panel, own, near, total, backs, outbox, inbox, row_factor, factor_a, factor_b, tile_a, tile_b,
+    near_panel, far_panel, own, near, total, backs, outbox, inbox, mate_out, mate_in, row_factor, factor_a, factor_b, tile_a, tile_b,
     inverse, sequence, cur_own, cur_in, cur_group, cur_all,
-    met, gather_send, gather_recv, back_send, back_recv, cur_send, cur_recv, all_send, all_recv,
+    met, gather_send, gather_recv, back_send, back_recv, cur_send, cur_recv, all_send, all_recv, mate_send, mate_recv,
 ):
-    members, tiles, width = outbox.shape[0], backs.shape[0] - 1, points_ref.shape[1]
+    tiles, width = backs.shape[0] - 1, points_ref.shape[1]
+    members = lax.axis_size("member")
     rows = members // QUAD
     close = NEAR * QUAD
+    single = SINGLE * QUAD
     g = lax.axis_index("group")
     m = lax.axis_index("member")
     y, quad = m // QUAD, lax.rem(m, QUAD)
@@ -244,16 +247,15 @@
         add_near(factor[0:8, :], tile)
         keep_back(t, tile)
 
-    def back_copy(position):
+    def back_copy(position, box, slot):
         return pltpu.make_async_remote_copy(
-            src_ref=outbox.at[position], dst_ref=inbox.at[m],
-            send_sem=back_send, recv_sem=back_recv,
+            src_ref=outbox.at[box], dst_ref=inbox.at[slot], send_sem=back_send, recv_sem=back_recv,
             device_id={"group": nxt, "member": member_at(position)}, device_id_type=MESH,
         )
 
     def give_back(position):
         outbox[position] = backs[inverse[position]]
-        back_copy(position).start()
+        back_copy(position, position, position // QUAD * QUAD + quad).start()
 
     prepare(block_near(0), factor_a)
     exponent(factor_a, tile_a)
@@ -266,8 +268,12 @@
         products(2 * u + 1, factor_b, tile_b)
         exponent(factor_a, tile_a)
         prepare(block(2 * u + 3), factor_b)
-        give_back(2 * u)
-        give_back(2 * u + 1)
+
+        @pl.when(2 * u < single)
+        def _():
+            give_back(2 * u)
+            give_back(2 * u + 1)
+
 
     early = 3
 
@@ -325,19 +331,39 @@
 
         lax.fori_loop(first, last, body, 0)
 
-    each(1, members, lambda i: cur_copy(i).start())
-
-    keep_back(tiles - 2, tile_a)
-    keep_back(tiles - 1, tile_b)
-    each(tiles - 2, members, lambda i: give_back(members - 1 + tiles - 2 - i))
-
-
     def whole(ref, send_sem, recv_sem):
         return pltpu.make_async_remote_copy(
             src_ref=ref, dst_ref=ref, send_sem=send_sem, recv_sem=recv_sem,
             device_id={"group": g, "member": mate}, device_id_type=MESH,
         )
 
+    each(1, members, lambda i: cur_copy(i).start())
+
+    keep_back(tiles - 2, tile_a)
+    keep_back(tiles - 1, tile_b)
+
+    core = lax.rem(quad, 2)
+    shared = (members - single) // 2
+
+    def hand_over(j):
+        mate_out[j] = backs[inverse[single + 2 * j + 1 - core]]
+        pltpu.make_async_remote_copy(
+            src_ref=mate_out.at[j], dst_ref=mate_in.at[j], send_sem=mate_send, recv_sem=mate_recv,
+            device_id={"group": g, "member": mate}, device_id_type=MESH,
+        ).start()
+
+    def give_sum(i):
+        j = shared - 1 - i
+        position = single + 2 * j + core
+        sums = backs[inverse[position]].astype(F32) + mate_in[j].astype(F32)
+        outbox[single + j] = sums.astype(BF16)
+        back_copy(position, single + j, single + j // 2 * 2 + quad // 2).start()
+
+    each(0, shared, hand_over)
+    whole(mate_in, mate_send, mate_recv).wait_recv()
+    each(0, shared, give_sum)
+
+
     rest = pl.ds(1, members - 1)
     whole(cur_in.at[rest], cur_send, cur_recv).wait_recv()
     cur_group[...] = jnp.sum(cur_in[...], 0)
@@ -347,13 +373,14 @@
     whole(near_panel, gather_send.at[0], gather_recv.at[0]).wait_send()
     whole(far_panel, gather_send.at[1], gather_recv.at[0]).wait_send()
     whole(cur_in.at[rest], cur_send, cur_recv).wait_send()
+    whole(mate_out, mate_send, mate_recv).wait_send()
     whole(outbox, back_send, back_recv).wait_send()
     others = cur_all.at[pl.ds(1, group_count - 1)]
     whole(others, all_send, all_recv).wait_send()
 
     whole(inbox, back_send, back_recv).wait_recv()
     share = inbox[0].astype(F32)
-    for k in range(1, members):
+    for k in range(1, inbox.shape[0]):
         share = share + inbox[k].astype(F32)
     product_ref[...] = total[...] + near[...] + jnp.concatenate((share[:8], share[8:]), 1)
 
@@ -365,6 +392,7 @@
     width, dims, rhs = points.shape[1], points.shape[0], probes.shape[0]
     members, groups, tiles = lax.axis_size("member"), lax.axis_size("group"), col_blocks.shape[2]
     rows = members // QUAD
+    boxes = (members + SINGLE * QUAD) // 2
     vmem = pl.BlockSpec(memory_space=pltpu.VMEM)
     dma = pltpu.SemaphoreType.DMA
     product, curvature = pl.pallas_call(
@@ -379,8 +407,8 @@
             pltpu.VMEM((rhs, width), F32),
             pltpu.VMEM((rhs, width), F32),
             pltpu.VMEM((tiles + 1, 16, width // 2), BF16),
-            pltpu.VMEM((members, 16, width // 2), BF16),
-            pltpu.VMEM((members, 16, width // 2), BF16),
+            *[pltpu.VMEM((boxes, 16, width // 2), BF16)] * 2,
+            *[pltpu.VMEM(((members - SINGLE * QUAD) // 2, 16, width // 2), BF16)] * 2,
             pltpu.VMEM((width, 48), BF16),
             pltpu.VMEM((48, width), BF16),
             pltpu.VMEM((48, width), BF16),
@@ -392,7 +420,7 @@
             pltpu.VMEM((1, 128), F32),
             pltpu.VMEM((groups, 1, 128), F32),
             pltpu.SemaphoreType.REGULAR((3,)), dma((2,)), dma((members,)),
-            dma, dma, dma, dma, dma, dma,
+            *[dma] * 8,
         ],
         compiler_params=pltpu.CompilerParams(
             collective_id=0, has_side_effects=True, vmem_limit_bytes=48 * 2**20

time: 76.6 us -> 75.3 us (0.983)
  Pallas kernels: 72.4 us -> 71.1 us
    pallas_call x1, Pallas kernels: 72.4 us -> 71.1 us  [body(): pl.pallas_call(functools.partial(kernel, dims, groups), out_shape=(jax.Sh...]
where the time goes in v4:
time: 75.3 us; the launch traced here: 75 us
  Pallas kernels  71.1 us (94%)
  local copies, waits for them, and re-layouts  3.25 us (4%)
    pallas_call x1, Pallas kernels, body(): pl.pallas_call(functools.partial(kernel, dims, groups), out_shape=(jax.Sh...  71.1 us
    unnamed x7, local copies, waits for them, and re-layouts  2.74 us

profile of v4, /device:TPU:1, one launch (start us, length us, event | category | flops | bytes accessed | tf_op | source)
XLA Modules:
  0.0 75.0 jit_solution(17816818036464959910)
XLA Ops:
  0.6 0.0 copy-start
  0.6 0.7 copy-done
  1.4 0.0 copy-start.1
  1.4 0.7 copy-done.1
  2.1 0.0 copy-start.2
  2.1 0.7 copy-done.2
  2.8 71.1 %shard_map.50 = (f32[8,1024]{1,0:T(8,128)S(1)}, f32[1,128]{1,0:T(1,128)S(1)}) custom-call(bf16[9,1024]{1,0:T(8,128)(2,1)S(1)} %copy-done, bf16[8,1024]{1,0:T(8,128)(2,1)S(1)} %copy-done.1, s32[1,1,20]{2,1,0:T(1,128)S(1)} %copy-done.2), custom_call_target="tpu_custom_call" | custom-call | tf_op jit(solution)/shard_map/pallas_call | solution.py:398
  73.9 0.5 slice_bitcast_fusion
  74.4 0.6 copy.6
Async XLA Ops:
  0.6 0.8 %copy-start = (bf16[9,1024]{1,0:T(8,128)(2,1)S(1)}, bf16[9,1024]{1,0:T(8,128)(2,1)}, u32[]{:S(2)}) copy-start(bf16[9,1024]{1,0:T(8,128)(2,1)} %points_ref.1) | copy-start | bytes 55300
  1.4 0.7 copy-start.1
  2.1 0.7 copy-start.2

commit v5 on v4

--- a/solution.py
+++ b/solution.py
@@ -15,7 +15,7 @@
 exponent_scale = 1.4426950408889634 / 3.0
 
 QUAD = 4
-ORDER = (2, -2, 3, -3, 0, 1, -1, 4)
+ORDER = (1, -1, 3, -3, 0, 2, -2, 4)
 HOME = ORDER.index(0)
 SINGLE = 4
 NEAR = 5
@@ -297,7 +297,7 @@
 
     lax.fori_loop(0, early, early_pair, 0)
     lax.fori_loop(early, tiles // 2 - 1, late_pair, 0)
-    add_near(factor_a[0:8, :], tile_a)
+    products(tiles - 2, factor_a, tile_a)
     exponent(factor_b, tile_b)
     add_near(factor_b[0:8, :], tile_b)
 
@@ -339,7 +339,6 @@
 
     each(1, members, lambda i: cur_copy(i).start())
 
-    keep_back(tiles - 2, tile_a)
     keep_back(tiles - 1, tile_b)
 
     core = lax.rem(quad, 2)

time: 75.3 us -> 75 us (level)
  no operation moved by 1% of the time
where the time goes in v5:
time: 75 us; the launch traced here: 74.7 us
  Pallas kernels  70.8 us (94%)
  local copies, waits for them, and re-layouts  3.25 us (4%)
    pallas_call x1, Pallas kernels, body(): pl.pallas_call(functools.partial(kernel, dims, groups), out_shape=(jax.Sh...  70.8 us
    unnamed x7, local copies, waits for them, and re-layouts  2.74 us

profile of v5, /device:TPU:1, one launch (start us, length us, event | category | flops | bytes accessed | tf_op | source)
XLA Modules:
  0.0 74.7 jit_solution(8122033335371560049)
XLA Ops:
  0.6 0.0 copy-start
  0.6 0.7 %copy-done = bf16[9,1024]{1,0:T(8,128)(2,1)S(1)} copy-done((bf16[9,1024]{1,0:T(8,128)(2,1)S(1)}, bf16[9,1024]{1,0:T(8,128)(2,1)}, u32[]{:S(2)}) %copy-start) | copy-done | bytes 18456
  1.4 0.0 copy-start.1
  1.4 0.7 copy-done.1
  2.1 0.0 copy-start.2
  2.1 0.7 copy-done.2
  2.8 70.8 %shard_map.50 = (f32[8,1024]{1,0:T(8,128)S(1)}, f32[1,128]{1,0:T(1,128)S(1)}) custom-call(bf16[9,1024]{1,0:T(8,128)(2,1)S(1)} %copy-done, bf16[8,1024]{1,0:T(8,128)(2,1)S(1)} %copy-done.1, s32[1,1,20]{2,1,0:T(1,128)S(1)} %copy-done.2), custom_call_target="tpu_custom_call" | custom-call | tf_op jit(solution)/shard_map/pallas_call | solution.py:397
  73.6 0.5 slice_bitcast_fusion
  74.1 0.6 copy.6
Async XLA Ops:
  0.6 0.8 %copy-start = (bf16[9,1024]{1,0:T(8,128)(2,1)S(1)}, bf16[9,1024]{1,0:T(8,128)(2,1)}, u32[]{:S(2)}) copy-start(bf16[9,1024]{1,0:T(8,128)(2,1)} %points_ref.1) | copy-start | bytes 55300
  1.4 0.7 copy-start.1
  2.1 0.7 copy-start.2

commit v6 on v5

--- a/solution.py
+++ b/solution.py
@@ -329,7 +329,7 @@
             step(i)
             return 0
 
-        lax.fori_loop(first, last, body, 0)
+        lax.fori_loop(first, last, body, 0, unroll=True)
 
     def whole(ref, send_sem, recv_sem):
         return pltpu.make_async_remote_copy(

time: 75 us -> 74.7 us (level)
  no operation moved by 1% of the time
where the time goes in v6:
time: 74.7 us; the launch traced here: 74.4 us
  Pallas kernels  70.5 us (94%)
  local copies, waits for them, and re-layouts  3.25 us (4%)
    pallas_call x1, Pallas kernels, body(): pl.pallas_call(functools.partial(kernel, dims, groups), out_shape=(jax.Sh...  70.5 us
    unnamed x7, local copies, waits for them, and re-layouts  2.74 us

profile of v6, /device:TPU:1, one launch (start us, length us, event | category | flops | bytes accessed | tf_op | source)
XLA Modules:
  0.0 74.4 jit_solution(17985867720546384127)
XLA Ops:
  0.6 0.0 copy-start
  0.6 0.7 %copy-done = bf16[9,1024]{1,0:T(8,128)(2,1)S(1)} copy-done((bf16[9,1024]{1,0:T(8,128)(2,1)S(1)}, bf16[9,1024]{1,0:T(8,128)(2,1)}, u32[]{:S(2)}) %copy-start) | copy-done | bytes 18456
  1.4 0.0 copy-start.1
  1.4 0.7 copy-done.1
  2.1 0.0 copy-start.2
  2.1 0.7 copy-done.2
  2.8 70.5 %shard_map.50 = (f32[8,1024]{1,0:T(8,128)S(1)}, f32[1,128]{1,0:T(1,128)S(1)}) custom-call(bf16[9,1024]{1,0:T(8,128)(2,1)S(1)} %copy-done, bf16[8,1024]{1,0:T(8,128)(2,1)S(1)} %copy-done.1, s32[1,1,20]{2,1,0:T(1,128)S(1)} %copy-done.2), custom_call_target="tpu_custom_call" | custom-call | tf_op jit(solution)/shard_map/pallas_call | solution.py:397
  73.3 0.5 slice_bitcast_fusion
  73.8 0.6 copy.6
Async XLA Ops:
  0.6 0.8 %copy-start = (bf16[9,1024]{1,0:T(8,128)(2,1)S(1)}, bf16[9,1024]{1,0:T(8,128)(2,1)}, u32[]{:S(2)}) copy-start(bf16[9,1024]{1,0:T(8,128)(2,1)} %points_ref.1) | copy-start | bytes 55300
  1.4 0.7 copy-start.1
  2.1 0.7 copy-start.2
